TPU v7x, 128 devices: a whole 4x4x4 slice. The times are simulated.
128 devices in a mesh: mem: 16 (over x, z_lo, core), lev: 8 (over y, z_hi).
Axes of the slice: x: 4, y: 4, z: 4 (z_hi: 2, z_lo: 2; z = z_hi * 2 + z_lo), core: 2. Of those that a mesh axis runs over, the one named last changes fastest.
Arguments:
- control_vec: float32 [256, 64, 8192], P('mem', 'lev'), may hold values from -6 to 6
- ens_perturb: bfloat16 [256, 3, 64, 8192], P(None, None, 'lev', 'mem'), may hold values from -6 to 6
- loc_blocks: bfloat16 [64, 9, 128, 128], replicated, may hold values from -0.1875 to 0.1875
- tile_index: int32 [64, 9], replicated, may hold values from 0 to 63, all different within a row
- obs_weight: bfloat16 [3, 64, 256], P(None, 'lev'), may hold values from -0.4375 to 0.4375
- channel_level_mask: int32 [64, 256], P('lev'), may hold values 0 or 1
- obs_precision: float32 [256, 8192], P(None, 'mem'), may hold values from 2 to 64
Outputs:
- hess_vec: float32 [256, 64, 8192], P('mem', 'lev')
Inputs may be any that keep to these rules, and one draw needn't show every extreme that they name: `tile_index`: each row names 9 different tiles; every tile is named by some row.
All inputs are finite; a program needn't handle non-finite values. No bound on the sum of `channel_level_mask` on one device may be relied on, other than what follows from the above.
Results may differ from a plain program's by a relative error of at most 0.012.
Values may be sent and summed in bfloat16 or wider, within the bound.
A program may use at most 192 MiB of HBM per device.

v0:
```python
import math
import jax
import jax.numpy as jnp
from jax import lax
from jax.sharding import PartitionSpec as P


def observe_adjoint(analysis_increment, operator, obs_precision):
    channels = operator.shape[2]
    share = channels // lax.axis_size("lev")
    operator_partial = operator
    local_similarity = lax.psum_scatter(
        jnp.einsum(
            "bws,bwn->sn", operator_partial, analysis_increment, preferred_element_type=jnp.float32
        ),
        "lev",
        scatter_dimension=0,
        tiled=True,
    )
    precision_rows = lax.dynamic_slice_in_dim(
        obs_precision, lax.axis_index("lev") * share, share, 0
    )
    weighted = (precision_rows * local_similarity).astype(jnp.bfloat16)
    operator_partial = operator
    gradient = jnp.einsum(
        "nhs,sb->nhb",
        operator_partial,
        lax.all_gather(weighted, "lev", axis=0, tiled=True),
        preferred_element_type=jnp.float32,
    )
    return gradient.astype(jnp.bfloat16)


def body(
    control_vec, ens_perturb, loc_blocks, tile_index, obs_weight, channel_level_mask, obs_precision
):
    mem_rows, lev_rows, points = control_vec.shape
    tile_len = loc_blocks.shape[2]
    tile_count = points // tile_len
    neighbours = tile_index.shape[1]
    row_total = mem_rows * lev_rows
    control_low = control_vec.astype(jnp.bfloat16).reshape(row_total, tile_count, tile_len)
    blocks = jnp.take(control_low, tile_index, axis=1)
    localized = jnp.einsum("rtkj,tkji->rti", blocks, loc_blocks, preferred_element_type=jnp.float32)
    localized = localized.astype(jnp.bfloat16).reshape(mem_rows, lev_rows, points)
    members = ens_perturb.shape[0]
    ens_scale = 1.0 / math.sqrt(members - 1)
    operator = obs_weight * channel_level_mask.astype(jnp.bfloat16)
    local_pts = lax.all_to_all(localized, "mem", split_axis=2, concat_axis=0, tiled=True)
    analysis_increment = jnp.einsum(
        "mvlp,mlp->vlp", ens_perturb, local_pts, preferred_element_type=jnp.float32
    )
    analysis_increment = (analysis_increment * ens_scale).astype(jnp.bfloat16)
    gradient = observe_adjoint(analysis_increment, operator, obs_precision)
    back_pts = jnp.einsum(
        "mvlp,vlp->mlp", ens_perturb, gradient, preferred_element_type=jnp.float32
    )
    back_pts = (back_pts * ens_scale).astype(jnp.bfloat16)
    backward_values = lax.all_to_all(back_pts, "mem", split_axis=0, concat_axis=2, tiled=True)
    back_tiles = backward_values.reshape(row_total, tile_count, tile_len)
    contrib = jnp.einsum(
        "rti,tkji->rtkj", back_tiles, loc_blocks, preferred_element_type=jnp.float32
    )
    contrib = contrib.reshape(row_total, tile_count * neighbours, tile_len)
    targets = tile_index.reshape(-1)
    adjoint = jnp.zeros((row_total, tile_count, tile_len), jnp.float32).at[:, targets].add(contrib)
    return control_vec + adjoint.reshape(mem_rows, lev_rows, points)


def solution(mesh):
    return jax.shard_map(
        body,
        mesh=mesh,
        in_specs=(
            P("mem", "lev", None),
            P(None, None, "lev", "mem"),
            P(),
            P(),
            P(None, "lev", None),
            P("lev", None),
            P(None, "mem"),
        ),
        out_specs=P("mem", "lev", None),
        check_vma=False,
    )
```

profile of v0, /device:TPU:33, one launch (start us, length us, event | category | flops | bytes accessed | tf_op | source)
XLA Modules:
  0.0 473.2 jit_solution(2274181088321798920)
XLA Ops:
  6.5 0.7 compare_and_fusion
  7.2 0.7 compare_select_fusion
  8.3 2.6 convert_bitcast_fusion
  11.5 1.4 copy.50
  12.8 15.9 %gather_fusion = bf16[576,128,128]{2,1,0:T(8,128)(2,1)} fusion(bf16[128,64,128]{2,0,1:T(8,128)(2,1)S(1)} %copy.50, s32[1024]{0:T(1024)S(1)} %pad_clamp_fusion), kind=kCustom, calls=%fused_computation | custom fusion | bytes 37751040 | tf_op jit(solution)/shard_map/jit(_take)/gather | solution.py:43
  28.8 14.5 %fusion.10 = bf16[128,64,128]{2,0,1:T(8,128)(2,1)S(1)} fusion(bf16[64,9,128,128]{3,2,1,0:T(8,128)(2,1)} %param.9, bf16[64,9,128,128]{3,2,1,0:T(8,128)(2,1)} %bitcast.64, pred[64,9]{1,0:T(8,128)(4,1)S(1)} %copy.48), kind=kOutput, calls=%fused_computation.16 | convolution fusion | flops 2426404864 | bytes 39846464 | tf_op jit(solution)/shard_map/rtkj,tkji->rti/dot_general | solution.py:44
  43.3 2.7 copy.51
  45.9 2.8 reshape.55
  48.8 13.3 %copy.52 = bf16[16,8,8192]{0,1,2:T(8,128)(2,1)} copy(bf16[16,8,8192]{2,1,0:T(8,128)(2,1)S(1)} %reshape.55) | data formatting | bytes 4194304 | tf_op jit(solution)/shard_map/reshape | solution.py:45
  62.1 20.8 %reshape.86 = bf16[16,2,32768]{2,1,0:T(2,128)(2,1)} reshape(bf16[8192,8,16]{2,1,0:T(8,128)(2,1)} %bitcast.62) | data formatting | bytes 4194304
  82.9 6.2 %all-to-all-start = ((bf16[16,2,32768]{2,1,0:T(2,128)(2,1)}), bf16[16,2,32768]{2,1,0:T(2,128)(2,1)S(1)}, u32[]{:S(2)}, u32[]{:S(2)}) async-start(bf16[16,2,32768]{2,1,0:T(2,128)(2,1)} %reshape.86), calls=%async_computation | async-start | bytes 4194304 | tf_op jit(solution)/shard_map/all_to_all | solution.py:49
  89.4 28.4 %all-to-all-done = bf16[16,2,32768]{2,1,0:T(2,128)(2,1)S(1)} async-done(((bf16[16,2,32768]{2,1,0:T(2,128)(2,1)}), bf16[16,2,32768]{2,1,0:T(2,128)(2,1)S(1)}, u32[]{:S(2)}, u32[]{:S(2)}) %all-to-all-start) | async-done | bytes 2097184 | tf_op jit(solution)/shard_map/all_to_all | solution.py:49
  117.7 14.4 %reshape.87 = bf16[8192,8,16]{2,1,0:T(8,128)(2,1)} reshape(bf16[16,2,32768]{2,1,0:T(2,128)(2,1)S(1)} %all-to-all-done) | data formatting | bytes 4194304
  132.1 17.5 %copy.76 = bf16[16,16,8,512]{3,2,1,0:T(8,128)(2,1)S(1)} copy(bf16[16,16,8,512]{1,2,3,0:T(8,128)(2,1)} %bitcast.63) | data formatting | bytes 4194304
  149.6 0.7 bitcast_convert_fusion.1
  150.3 4.4 multiply_reduce_fusion.1
  154.7 1.1 convolution_bitcast_fusion
  155.8 68.2 %reduce-scatter.2.cloned.1.call-done = f32[32,512]{1,0:T(8,128)} async-done(((f32[256,512]{1,0:T(8,128)}), f32[32,512]{1,0:T(8,128)}) %reduce-scatter.2.cloned.1.call-update) | async-done | bytes 65552 | tf_op jit(solution)/shard_map/reduce_scatter | solution.py:12
  224.1 0.9 multiply_convert_fusion.1
  224.9 28.1 %all_gather.3 = bf16[256,512]{1,0:T(8,128)(2,1)S(1)} all-gather(bf16[32,512]{1,0:T(8,128)(2,1)S(1)} %multiply_convert_fusion.1), channel_id=1, replica_groups=mesh['mem'=16,'lev'=8] {'lev'}, dimensions={0}, use_global_device_ids=true | all-gather | bytes 294912 | tf_op jit(solution)/shard_map/all_gather | solution.py:28
  253.2 5.5 %multiply_reduce_fusion = f32[8,512,256]{1,0,2:T(8,128)S(1)} fusion(f32[8,512,3]{1,0,2:T(8,128)S(1)} %fusion.14, bf16[256,3,8,512]{3,2,1,0:T(8,128)(2,1)} %param.8), kind=kLoop, calls=%fused_computation.6 | loop fusion | flops 8388608 | bytes 10534912 | tf_op jit(solution)/shard_map/mvlp,vlp->mlp/dot_general | solution.py:55
  258.7 2.0 fusion.7
  260.7 14.2 %all-to-all-start.1 = ((bf16[256,8,512]{2,1,0:T(8,128)(2,1)}), bf16[256,8,512]{2,1,0:T(8,128)(2,1)S(1)}, u32[]{:S(2)}, u32[]{:S(2)}) async-start(bf16[256,8,512]{2,1,0:T(8,128)(2,1)} %fusion.7), calls=%async_computation.2 | async-start | bytes 4194304 | tf_op jit(solution)/shard_map/all_to_all | solution.py:59
  275.2 28.4 %all-to-all-done.1 = bf16[256,8,512]{2,1,0:T(8,128)(2,1)S(1)} async-done(((bf16[256,8,512]{2,1,0:T(8,128)(2,1)}), bf16[256,8,512]{2,1,0:T(8,128)(2,1)S(1)}, u32[]{:S(2)}, u32[]{:S(2)}) %all-to-all-start.1) | async-done | bytes 2097184 | tf_op jit(solution)/shard_map/all_to_all | solution.py:59
  303.5 2.5 copy.55
  306.0 3.1 reshape.56
  309.1 20.8 %fusion.8 = f32[64,128,9,128]{3,1,2,0:T(8,128)} fusion(bf16[64,9,128,128]{3,2,1,0:T(8,128)(2,1)} %param.9, bf16[128,64,128,1]{2,1,0,3:T(8,128)(2,1)S(1)} %bitcast.65), kind=kOutput, calls=%fused_computation.12 | convolution fusion | flops 2415919104 | bytes 58720256 | tf_op jit(solution)/shard_map/rti,tkji->rtkj/dot_general | solution.py:61
  329.9 2.5 broadcast_in_dim.17
  332.4 116.4 %scatter_fusion = f32[128,64,128]{2,0,1:T(8,128)} fusion(f32[128,64,128]{2,0,1:T(8,128)} %broadcast_in_dim.17, s32[576]{0:T(1024)S(1)} %fusion.23, f32[576,128,128]{2,1,0:T(8,128)} %bitcast.61), kind=kCustom, calls=%fused_computation.1 | custom fusion | flops 9437184 | bytes 113248512 | tf_op jit(solution)/shard_map/scatter-add | solution.py:66
  448.9 6.5 %copy.57 = f32[128,64,128]{2,1,0:T(8,128)} copy(f32[128,64,128]{2,0,1:T(8,128)} %scatter_fusion) | data formatting | bytes 8388608 | tf_op jit(solution)/shard_map/scatter-add | solution.py:66
  455.4 4.9 %reshape.58 = f32[16,8,8192]{2,1,0:T(8,128)} reshape(f32[128,64,128]{2,1,0:T(8,128)} %copy.57) | data formatting | bytes 8388608 | tf_op jit(solution)/shard_map/reshape | solution.py:67
  460.4 6.0 %add.36 = f32[16,8,8192]{2,1,0:T(8,128)} add(f32[16,8,8192]{2,1,0:T(8,128)} %param.7, f32[16,8,8192]{2,1,0:T(8,128)} %reshape.58) | non-fusion elementwise | flops 1048576 | bytes 12582912 | tf_op jit(solution)/shard_map/add | solution.py:67
  (18 shorter events, 1.6 us)
Async XLA Ops:
  82.9 6.5 %copy-start.2 = (s32[8,256]{1,0:T(8,128)S(1)}, s32[8,256]{1,0:T(8,128)}, u32[]{:S(2)}) copy-start(s32[8,256]{1,0:T(8,128)} %param.12) | copy-start | bytes 24580
  82.9 34.9 %all-to-all-start = ((bf16[16,2,32768]{2,1,0:T(2,128)(2,1)}), bf16[16,2,32768]{2,1,0:T(2,128)(2,1)S(1)}, u32[]{:S(2)}, u32[]{:S(2)}) async-start(bf16[16,2,32768]{2,1,0:T(2,128)(2,1)} %reshape.86), calls=%async_computation | async-start | bytes 4194304 | tf_op jit(solution)/shard_map/all_to_all | solution.py:49
  89.1 134.9 %reduce-scatter.2.cloned.1.call-start = ((), (), s32[]{:S(2)}) async-start(), calls=%async_computation.3 | async-start | bytes 589824 | tf_op jit(solution)/shard_map/reduce_scatter | solution.py:12
  150.3 4.4 copy-start.1
  258.7 16.2 %copy-start = (s32[64,9]{0,1:T(8,128)S(1)}, s32[64,9]{0,1:T(8,128)}, u32[]{:S(2)}) copy-start(s32[64,9]{0,1:T(8,128)} %param.10) | copy-start | bytes 6916
  260.7 42.9 %all-to-all-start.1 = ((bf16[256,8,512]{2,1,0:T(8,128)(2,1)}), bf16[256,8,512]{2,1,0:T(8,128)(2,1)S(1)}, u32[]{:S(2)}, u32[]{:S(2)}) async-start(bf16[256,8,512]{2,1,0:T(8,128)(2,1)} %fusion.7), calls=%async_computation.2 | async-start | bytes 4194304 | tf_op jit(solution)/shard_map/all_to_all | solution.py:59
Sparse Core Ops, SparseCore 0:
  155.9 68.0 reduce-scatter.1
where the time goes:
time: 476 us; the launch traced here: 473 us
  other arithmetic  140 us (29%)
  waiting for transfers between devices  125 us (26%)
  local copies, waits for them, and re-layouts  109 us (23%)
  matrix products  36.5 us (8%)
  blocking collectives  28.1 us (6%)
  starting transfers between devices  20.7 us (4%)
  between operations  13.5 us (3%)
    scatter-add x1, other arithmetic, body(): jnp.zeros((row_total, tile_count, tile_len), jnp.float32).at[:, targets]  116 us
    reduce_scatter x1, waiting for transfers between devices, observe_adjoint(): lax.psum_scatter(jnp.einsum('bws,bwn->sn', operator_partial, analysis_inc...  68.2 us
    unnamed x11, local copies, waits for them, and re-layouts  53.3 us
    all_to_all x1, waiting for transfers between devices, body(): lax.all_to_all(localized, 'mem', split_axis=2, concat_axis=0, tiled=True)  28.4 us
    all_to_all x1, waiting for transfers between devices, body(): lax.all_to_all(back_pts, 'mem', split_axis=0, concat_axis=2, tiled=True)  28.4 us
    all_gather x1, blocking collectives, observe_adjoint(): lax.all_gather(weighted, 'lev', axis=0, tiled=True)  28.1 us
    dot_general x1, matrix products, body(): jnp.einsum('rti,tkji->rtkj', back_tiles, loc_blocks, preferred_element_ty...  20.8 us
    reshape x2, local copies, waits for them, and re-layouts, body(): localized.astype(jnp.bfloat16).reshape(mem_rows, lev_rows, points)  16.1 us
  transfers between devices with their start and end apart: 3, of which 3 were waited for; matrix products, arithmetic and copies ran while one was open for 0% of the time, Pallas kernels for 0%

commit v1 on v0

--- a/solution.py
+++ b/solution.py
@@ -3,6 +3,7 @@
 import jax.numpy as jnp
 from jax import lax
 from jax.sharding import PartitionSpec as P
+from jax.lax import all_to_all, axis_size
 
 
 def observe_adjoint(analysis_increment, operator, obs_precision):
@@ -25,7 +26,15 @@
     gradient = jnp.einsum(
         "nhs,sb->nhb",
         operator_partial,
-        lax.all_gather(weighted, "lev", axis=0, tiled=True),
+        jnp.concatenate(
+            all_to_all(
+                jnp.stack([weighted] * axis_size("lev")),
+                axis_name="lev",
+                split_axis=0,
+                concat_axis=0,
+            ),
+            0,
+        ),
         preferred_element_type=jnp.float32,
     )
     return gradient.astype(jnp.bfloat16)

time: 476 us -> 454 us (0.954)
  blocking collectives: 28.1 us -> 11.5 us
  starting transfers between devices: 20.7 us -> 15.6 us
    all_gather x1 -> x0, blocking collectives: 28.1 us -> none  [observe_adjoint(): lax.all_gather(weighted, 'lev', axis=0, tiled=True)]
    all_to_all x0 -> x1, blocking collectives: none -> 11.5 us  [observe_adjoint(): all_to_all(jnp.stack([weighted] * axis_size('lev')), axis_name='lev', spl...]
    all_to_all x1, starting transfers between devices: 14.2 us -> 9.13 us  [body(): lax.all_to_all(back_pts, 'mem', split_axis=0, concat_axis=2, tiled=True)]
where the time goes in v1:
time: 454 us; the launch traced here: 451 us
  other arithmetic  140 us (31%)
  waiting for transfers between devices  125 us (28%)
  local copies, waits for them, and re-layouts  109 us (24%)
  matrix products  36.5 us (8%)
  starting transfers between devices  15.6 us (3%)
  between operations  13.5 us (3%)
  blocking collectives  11.5 us (3%)
    scatter-add x1, other arithmetic, body(): jnp.zeros((row_total, tile_count, tile_len), jnp.float32).at[:, targets]  116 us
    reduce_scatter x1, waiting for transfers between devices, observe_adjoint(): lax.psum_scatter(jnp.einsum('bws,bwn->sn', operator_partial, analysis_inc...  68.2 us
    unnamed x11, local copies, waits for them, and re-layouts  53.3 us
    all_to_all x1, waiting for transfers between devices, body(): lax.all_to_all(localized, 'mem', split_axis=2, concat_axis=0, tiled=True)  28.4 us
    all_to_all x1, waiting for transfers between devices, body(): lax.all_to_all(back_pts, 'mem', split_axis=0, concat_axis=2, tiled=True)  28.4 us
    dot_general x1, matrix products, body(): jnp.einsum('rti,tkji->rtkj', back_tiles, loc_blocks, preferred_element_ty...  20.8 us
    reshape x2, local copies, waits for them, and re-layouts, body(): localized.astype(jnp.bfloat16).reshape(mem_rows, lev_rows, points)  16.1 us
    gather x1, local copies, waits for them, and re-layouts, body(): blocks = jnp.take(control_low, tile_index, axis=1)  15.9 us
  transfers between devices with their start and end apart: 3, of which 3 were waited for; matrix products, arithmetic and copies ran while one was open for 0% of the time, Pallas kernels for 0%

profile of v1, /device:TPU:33, one launch (start us, length us, event | category | flops | bytes accessed | tf_op | source)
XLA Modules:
  0.0 451.5 jit_solution(2648715788749510991)
XLA Ops:
  6.5 0.7 compare_and_fusion
  7.2 0.7 compare_select_fusion
  8.3 2.6 convert_bitcast_fusion
  11.5 1.4 copy.50
  12.8 15.9 %gather_fusion = bf16[576,128,128]{2,1,0:T(8,128)(2,1)} fusion(bf16[128,64,128]{2,0,1:T(8,128)(2,1)S(1)} %copy.50, s32[1024]{0:T(1024)S(1)} %pad_clamp_fusion), kind=kCustom, calls=%fused_computation | custom fusion | bytes 37751040 | tf_op jit(solution)/shard_map/jit(_take)/gather | solution.py:52
  28.8 14.5 %fusion.10 = bf16[128,64,128]{2,0,1:T(8,128)(2,1)S(1)} fusion(bf16[64,9,128,128]{3,2,1,0:T(8,128)(2,1)} %param.9, bf16[64,9,128,128]{3,2,1,0:T(8,128)(2,1)} %bitcast.65, pred[64,9]{1,0:T(8,128)(4,1)S(1)} %copy.48), kind=kOutput, calls=%fused_computation.16 | convolution fusion | flops 2426404864 | bytes 39846464 | tf_op jit(solution)/shard_map/rtkj,tkji->rti/dot_general | solution.py:53
  43.3 2.7 copy.51
  45.9 2.8 reshape.60
  48.8 13.3 %copy.52 = bf16[16,8,8192]{0,1,2:T(8,128)(2,1)} copy(bf16[16,8,8192]{2,1,0:T(8,128)(2,1)S(1)} %reshape.60) | data formatting | bytes 4194304 | tf_op jit(solution)/shard_map/reshape | solution.py:54
  62.1 20.8 %reshape.92 = bf16[16,2,32768]{2,1,0:T(2,128)(2,1)} reshape(bf16[8192,8,16]{2,1,0:T(8,128)(2,1)} %bitcast.63) | data formatting | bytes 4194304
  82.9 6.2 %all-to-all-start = ((bf16[16,2,32768]{2,1,0:T(2,128)(2,1)}), bf16[16,2,32768]{2,1,0:T(2,128)(2,1)S(1)}, u32[]{:S(2)}, u32[]{:S(2)}) async-start(bf16[16,2,32768]{2,1,0:T(2,128)(2,1)} %reshape.92), calls=%async_computation | async-start | bytes 4194304 | tf_op jit(solution)/shard_map/all_to_all | solution.py:58
  89.4 28.4 %all-to-all-done = bf16[16,2,32768]{2,1,0:T(2,128)(2,1)S(1)} async-done(((bf16[16,2,32768]{2,1,0:T(2,128)(2,1)}), bf16[16,2,32768]{2,1,0:T(2,128)(2,1)S(1)}, u32[]{:S(2)}, u32[]{:S(2)}) %all-to-all-start) | async-done | bytes 2097184 | tf_op jit(solution)/shard_map/all_to_all | solution.py:58
  117.7 14.4 %reshape.93 = bf16[8192,8,16]{2,1,0:T(8,128)(2,1)} reshape(bf16[16,2,32768]{2,1,0:T(2,128)(2,1)S(1)} %all-to-all-done) | data formatting | bytes 4194304
  132.1 17.5 %copy.76 = bf16[16,16,8,512]{3,2,1,0:T(8,128)(2,1)S(1)} copy(bf16[16,16,8,512]{1,2,3,0:T(8,128)(2,1)} %bitcast.64) | data formatting | bytes 4194304
  149.6 0.7 bitcast_convert_fusion.1
  150.3 4.4 multiply_reduce_fusion.1
  154.7 1.1 convolution_bitcast_fusion
  155.8 68.2 %reduce-scatter.2.cloned.1.call-done = f32[32,512]{1,0:T(8,128)} async-done(((f32[256,512]{1,0:T(8,128)}), f32[32,512]{1,0:T(8,128)}) %reduce-scatter.2.cloned.1.call-update) | async-done | bytes 65552 | tf_op jit(solution)/shard_map/reduce_scatter | solution.py:13
  224.1 0.9 multiply_convert_fusion.1
  225.0 11.5 %all_to_all.38 = bf16[8,32,512]{2,1,0:T(8,128)(2,1)S(1)} all-to-all(bf16[8,32,512]{2,1,0:T(8,128)(2,1)S(1)} %stack.2), channel_id=1, replica_groups=mesh['mem'=16,'lev'=8] {'lev'}, dimensions={0} | all-to-all | bytes 524288 | tf_op jit(solution)/shard_map/all_to_all | solution.py:30
  236.6 5.5 %multiply_reduce_fusion = f32[8,512,256]{1,0,2:T(8,128)S(1)} fusion(f32[8,512,3]{1,0,2:T(8,128)S(1)} %fusion.14, bf16[256,3,8,512]{3,2,1,0:T(8,128)(2,1)} %param.8), kind=kLoop, calls=%fused_computation.6 | loop fusion | flops 8388608 | bytes 10534912 | tf_op jit(solution)/shard_map/mvlp,vlp->mlp/dot_general | solution.py:64
  242.1 2.0 fusion.7
  244.1 9.1 %all-to-all-start.2 = ((bf16[256,8,512]{2,1,0:T(8,128)(2,1)}), bf16[256,8,512]{2,1,0:T(8,128)(2,1)S(1)}, u32[]{:S(2)}, u32[]{:S(2)}) async-start(bf16[256,8,512]{2,1,0:T(8,128)(2,1)} %fusion.7), calls=%async_computation.3 | async-start | bytes 4194304 | tf_op jit(solution)/shard_map/all_to_all | solution.py:68
  253.5 28.4 %all-to-all-done.2 = bf16[256,8,512]{2,1,0:T(8,128)(2,1)S(1)} async-done(((bf16[256,8,512]{2,1,0:T(8,128)(2,1)}), bf16[256,8,512]{2,1,0:T(8,128)(2,1)S(1)}, u32[]{:S(2)}, u32[]{:S(2)}) %all-to-all-start.2) | async-done | bytes 2097184 | tf_op jit(solution)/shard_map/all_to_all | solution.py:68
  281.8 2.5 copy.55
  284.3 3.1 reshape.62
  287.4 20.8 %fusion.8 = f32[64,128,9,128]{3,1,2,0:T(8,128)} fusion(bf16[64,9,128,128]{3,2,1,0:T(8,128)(2,1)} %param.9, bf16[128,64,128,1]{2,1,0,3:T(8,128)(2,1)S(1)} %bitcast.66), kind=kOutput, calls=%fused_computation.12 | convolution fusion | flops 2415919104 | bytes 58720256 | tf_op jit(solution)/shard_map/rti,tkji->rtkj/dot_general | solution.py:70
  308.2 2.5 broadcast_in_dim.17
  310.7 116.4 %scatter_fusion = f32[128,64,128]{2,0,1:T(8,128)} fusion(f32[128,64,128]{2,0,1:T(8,128)} %broadcast_in_dim.17, s32[576]{0:T(1024)S(1)} %fusion.22, f32[576,128,128]{2,1,0:T(8,128)} %bitcast.62), kind=kCustom, calls=%fused_computation.1 | custom fusion | flops 9437184 | bytes 113248512 | tf_op jit(solution)/shard_map/scatter-add | solution.py:75
  427.2 6.5 %copy.57 = f32[128,64,128]{2,1,0:T(8,128)} copy(f32[128,64,128]{2,0,1:T(8,128)} %scatter_fusion) | data formatting | bytes 8388608 | tf_op jit(solution)/shard_map/scatter-add | solution.py:75
  433.7 4.9 %reshape.64 = f32[16,8,8192]{2,1,0:T(8,128)} reshape(f32[128,64,128]{2,1,0:T(8,128)} %copy.57) | data formatting | bytes 8388608 | tf_op jit(solution)/shard_map/reshape | solution.py:76
  438.7 6.0 %add.36 = f32[16,8,8192]{2,1,0:T(8,128)} add(f32[16,8,8192]{2,1,0:T(8,128)} %param.7, f32[16,8,8192]{2,1,0:T(8,128)} %reshape.64) | non-fusion elementwise | flops 1048576 | bytes 12582912 | tf_op jit(solution)/shard_map/add | solution.py:76
  (19 shorter events, 1.6 us)
Async XLA Ops:
  82.9 6.5 %copy-start.2 = (s32[8,256]{1,0:T(8,128)S(1)}, s32[8,256]{1,0:T(8,128)}, u32[]{:S(2)}) copy-start(s32[8,256]{1,0:T(8,128)} %param.12) | copy-start | bytes 24580
  82.9 34.9 %all-to-all-start = ((bf16[16,2,32768]{2,1,0:T(2,128)(2,1)}), bf16[16,2,32768]{2,1,0:T(2,128)(2,1)S(1)}, u32[]{:S(2)}, u32[]{:S(2)}) async-start(bf16[16,2,32768]{2,1,0:T(2,128)(2,1)} %reshape.92), calls=%async_computation | async-start | bytes 4194304 | tf_op jit(solution)/shard_map/all_to_all | solution.py:58
  89.1 134.9 %reduce-scatter.2.cloned.1.call-start = ((), (), s32[]{:S(2)}) async-start(), calls=%async_computation.4 | async-start | bytes 589824 | tf_op jit(solution)/shard_map/reduce_scatter | solution.py:13
  150.3 4.4 copy-start.1
  242.1 11.1 %copy-start = (s32[64,9]{0,1:T(8,128)S(1)}, s32[64,9]{0,1:T(8,128)}, u32[]{:S(2)}) copy-start(s32[64,9]{0,1:T(8,128)} %param.10) | copy-start | bytes 6916
  244.1 37.8 %all-to-all-start.2 = ((bf16[256,8,512]{2,1,0:T(8,128)(2,1)}), bf16[256,8,512]{2,1,0:T(8,128)(2,1)S(1)}, u32[]{:S(2)}, u32[]{:S(2)}) async-start(bf16[256,8,512]{2,1,0:T(8,128)(2,1)} %fusion.7), calls=%async_computation.3 | async-start | bytes 4194304 | tf_op jit(solution)/shard_map/all_to_all | solution.py:68
Sparse Core Ops, SparseCore 0:
  155.9 68.0 reduce-scatter.1
